TPU v7x, 128 devices: a whole 4x4x4 slice. The times are simulated.
128 devices in a mesh: dp: 16 (over z, x_hi, core), tensor: 8 (over x_lo, y).
Axes of the slice: x: 4 (x_hi: 2, x_lo: 2; x = x_hi * 2 + x_lo), y: 4, z: 4, core: 2. Of those that a mesh axis runs over, the one named last changes fastest.
Arguments:
- inputs: float32 [32768, 1024], P(('dp', 'tensor')), may hold values from -6 to 6
- lengths: int32 [16, 4], P('dp'), may hold values from 1 to 1024, 2048 in all within a row
- ln1_gain: float32 [1024], replicated, may hold values from 0.1 to 1.9
- ln1_bias: float32 [1024], replicated, may hold values from -1.75 to 1.75
- ln2_gain: float32 [1024], replicated, may hold values from 0.1 to 1.9
- ln2_bias: float32 [1024], replicated, may hold values from -1.75 to 1.75
- w_query: float32 [1024, 1024], P('dp', 'tensor'), may hold values from -0.1875 to 0.1875
- w_key: float32 [1024, 1024], P('dp', 'tensor'), may hold values from -0.1875 to 0.1875
- w_value: float32 [1024, 1024], P('dp', 'tensor'), may hold values from -0.1875 to 0.1875
- w_out: float32 [1024, 1024], P('tensor', 'dp'), may hold values from -1.5 to 1.5
- w_up: float32 [1024, 4096], P('dp', 'tensor'), may hold values from -0.1875 to 0.1875
- w_down: float32 [4096, 1024], P('tensor', 'dp'), may hold values from -0.09375 to 0.09375
- cotangent: float32 [32768, 1024], P(('dp', 'tensor')), may hold values from -6 to 6
Outputs:
- result: float32 [32768, 1024], P(('dp', 'tensor'))
- grad_inputs: float32 [32768, 1024], P(('dp', 'tensor'))
- grad_ln1_gain: float32 [1024], replicated
- grad_ln1_bias: float32 [1024], replicated
- grad_ln2_gain: float32 [1024], replicated
- grad_ln2_bias: float32 [1024], replicated
- grad_w_query: float32 [1024, 1024], P('dp', 'tensor')
- grad_w_key: float32 [1024, 1024], P('dp', 'tensor')
- grad_w_value: float32 [1024, 1024], P('dp', 'tensor')
- grad_w_out: float32 [1024, 1024], P('tensor', 'dp')
- grad_w_up: float32 [1024, 4096], P('dp', 'tensor')
- grad_w_down: float32 [4096, 1024], P('tensor', 'dp')
Inputs may be any that keep to these rules, and one draw needn't show every extreme that they name: The 4 lengths of a row sum to 2048; one of them is 1024.
All inputs are finite; a program needn't handle non-finite values.
Results may differ from a plain program's by a relative error of at most 0.025.
Values may be sent and summed in bfloat16 or wider, within the bound.
No kernel may reach another device: no remote copies, remote signals or barrier semaphores. Data moves between devices by JAX's collectives and lax.ppermute only.
A program may use at most 128 MiB of HBM per device.

v0:
```python
import jax
import jax.numpy as jnp
from jax import lax
from jax.sharding import PartitionSpec as P

HEAD_DIM = 64


precise = lax.Precision.HIGHEST
norm_eps = 1e-05


def layer_norm(values, norm_gain, norm_shift):
    center = jnp.mean(values, axis=-1, keepdims=True)
    centred = values - center
    spread = jnp.mean(centred * centred, axis=-1, keepdims=True)
    return centred * lax.rsqrt(spread + norm_eps) * norm_gain + norm_shift


def feature(values):
    return jax.nn.elu(values) + 1.0


def gelu_exact(values):
    return jax.nn.gelu(values, approximate=False)


def segment_ids(lengths, positions):
    item_ends = jnp.cumsum(lengths)
    places = jnp.arange(positions, dtype=jnp.int32)
    return jnp.sum((places[:, None] >= item_ends[None, :]).astype(jnp.int32), axis=1)


def with_transposed(left, right):
    return lax.dot_general(
        left, right, (((1,), (1,)), ((), ())), preferred_element_type=jnp.float32
    )


def transposed_with(left, right):
    return lax.dot_general(
        left, right, (((0,), (0,)), ((), ())), preferred_element_type=jnp.float32
    )


def block_terms(queries, keys_in, values_in, segments, previous, memory, totals):
    block_len = segments.shape[0]
    places = jnp.arange(block_len, dtype=jnp.int32)
    allowed = (
        (places[:, None] >= places[None, :]) & (segments[:, None] == segments[None, :])
    ).astype(jnp.float32)
    scores = jnp.einsum("ihe,jhe->hij", queries, keys_in, precision=precise) * allowed[None]
    carried = (segments == previous).astype(jnp.float32)
    numerator = jnp.einsum("hij,jhe->ihe", scores, values_in, precision=precise)
    numerator = numerator + carried[:, None, None] * jnp.einsum(
        "ihe,hef->ihf", queries, memory, precision=precise
    )
    denominator = jnp.sum(scores, axis=2).T + carried[:, None] * jnp.einsum(
        "ihe,he->ih", queries, totals, precision=precise
    )
    attended = numerator / denominator[:, :, None]
    return (allowed, scores, carried, denominator, attended)


def block_forward(carry, block):
    memory, totals, previous = carry
    raw_query, raw_key, raw_value, segments = block
    queries = raw_query.astype(jnp.float32)
    keys_in = raw_key.astype(jnp.float32)
    values_in = raw_value.astype(jnp.float32)
    allowed, scores, carried, denominator, attended = block_terms(
        queries, keys_in, values_in, segments, previous, memory, totals
    )
    last_seg = segments[-1]
    survive = (last_seg == previous).astype(jnp.float32)
    in_last = (segments == last_seg).astype(jnp.float32)[:, None, None]
    new_memory = survive * memory + jnp.einsum(
        "jhe,jhf->hef", keys_in * in_last, values_in, precision=precise
    )
    new_totals = survive * totals + jnp.sum(keys_in * in_last, axis=0)
    return ((new_memory, new_totals, last_seg), (attended, memory, totals))


def block_backward(carry, block):
    grad_memory, grad_totals = carry
    raw_query, raw_key, raw_value, raw_grad, segments, previous, memory, totals = block
    queries = raw_query.astype(jnp.float32)
    keys_in = raw_key.astype(jnp.float32)
    values_in = raw_value.astype(jnp.float32)
    grad_out = raw_grad.astype(jnp.float32)
    allowed, scores, carried, denominator, attended = block_terms(
        queries, keys_in, values_in, segments, previous, memory, totals
    )
    last_seg = segments[-1]
    survive = (last_seg == previous).astype(jnp.float32)
    in_last = (segments == last_seg).astype(jnp.float32)[:, None, None]
    grad_numer = grad_out / denominator[:, :, None]
    grad_denom = -jnp.sum(grad_out * attended, axis=2) / denominator
    grad_scores = (
        jnp.einsum("ihe,jhe->hij", grad_numer, values_in, precision=precise)
        + grad_denom.T[:, :, None]
    ) * allowed[None]
    grad_values = jnp.einsum("hij,ihe->jhe", scores, grad_numer, precision=precise)
    grad_values = grad_values + in_last * jnp.einsum(
        "jhe,hef->jhf", keys_in, grad_memory, precision=precise
    )
    grad_keys = jnp.einsum("hij,ihe->jhe", grad_scores, queries, precision=precise)
    grad_keys = grad_keys + in_last * (
        jnp.einsum("jhf,hef->jhe", values_in, grad_memory, precision=precise) + grad_totals[None]
    )
    grad_queries = jnp.einsum("hij,jhe->ihe", grad_scores, keys_in, precision=precise)
    grad_queries = grad_queries + carried[:, None, None] * (
        jnp.einsum("ihf,hef->ihe", grad_numer, memory, precision=precise)
        + grad_denom[:, :, None] * totals[None]
    )
    weighted = queries * carried[:, None, None]
    new_memory = survive * grad_memory + jnp.einsum(
        "ihe,ihf->hef", weighted, grad_numer, precision=precise
    )
    new_totals = survive * grad_totals + jnp.einsum(
        "ihe,ih->he", weighted, grad_denom, precision=precise
    )
    return ((new_memory, new_totals), (grad_queries, grad_keys, grad_values))


def local(
    inputs,
    lengths,
    ln1_gain,
    ln1_bias,
    ln2_gain,
    ln2_bias,
    w_query,
    w_key,
    w_value,
    w_out,
    w_up,
    w_down,
    cotangent,
):
    local_rows = inputs.shape[0]
    seq_len = local_rows * lax.axis_size("tensor")
    head_cols = w_query.shape[1]
    heads_here = head_cols // HEAD_DIM
    block_len = min(512, seq_len)
    blocks = seq_len // block_len
    query_low = w_query.astype(jnp.bfloat16)
    key_low = w_key.astype(jnp.bfloat16)
    value_low = w_value.astype(jnp.bfloat16)
    out_low = w_out.astype(jnp.bfloat16)
    up_low = w_up.astype(jnp.bfloat16)
    down_low = w_down.astype(jnp.bfloat16)
    query_full, key_full, value_full, out_full, up_full, down_full = (
        lax.all_gather(query_low, "dp", axis=0, tiled=True),
        lax.all_gather(key_low, "dp", axis=0, tiled=True),
        lax.all_gather(value_low, "dp", axis=0, tiled=True),
        lax.all_gather(out_low, "dp", axis=1, tiled=True),
        lax.all_gather(up_low, "dp", axis=0, tiled=True),
        lax.all_gather(down_low, "dp", axis=1, tiled=True),
    )
    segments = segment_ids(lengths[0], seq_len)
    segment_blocks = segments.reshape(blocks, block_len)
    previous_all = jnp.concatenate([jnp.full((1,), -1, jnp.int32), segment_blocks[:-1, -1]])
    normed_one, norm_one_pull = jax.vjp(layer_norm, inputs, ln1_gain, ln1_bias)
    first_all = lax.all_gather(normed_one.astype(jnp.bfloat16), "tensor", axis=0, tiled=True)
    queries = jnp.dot(first_all, query_full, preferred_element_type=jnp.float32)
    key_proj = jnp.dot(first_all, key_full, preferred_element_type=jnp.float32)
    values_low = jnp.dot(first_all, value_full, preferred_element_type=jnp.float32).astype(
        jnp.bfloat16
    )
    feat_query32, query_pull = jax.vjp(feature, queries)
    feat_key32, key_pull = jax.vjp(feature, key_proj)
    feat_query = feat_query32.astype(jnp.bfloat16)
    feat_key = feat_key32.astype(jnp.bfloat16)

    def to_blocks(values):
        return values.reshape(blocks, block_len, heads_here, HEAD_DIM)

    initial = (
        jnp.zeros((heads_here, HEAD_DIM, HEAD_DIM), jnp.float32),
        jnp.zeros((heads_here, HEAD_DIM), jnp.float32),
        jnp.array(-1, jnp.int32),
    )
    unused, (attended, memories, totals_all) = lax.scan(
        block_forward,
        initial,
        (to_blocks(feat_query), to_blocks(feat_key), to_blocks(values_low), segment_blocks),
    )
    attended_low = attended.reshape(seq_len, head_cols).astype(jnp.bfloat16)
    hidden = inputs + lax.psum_scatter(
        jnp.dot(attended_low, out_full, preferred_element_type=jnp.float32).astype(jnp.bfloat16),
        "tensor",
        scatter_dimension=0,
        tiled=True,
    ).astype(jnp.float32)
    normed_two, norm_two_pull = jax.vjp(layer_norm, hidden, ln2_gain, ln2_bias)
    second_all = lax.all_gather(normed_two.astype(jnp.bfloat16), "tensor", axis=0, tiled=True)
    up_proj = jnp.dot(second_all, up_full, preferred_element_type=jnp.float32)
    activated32, gelu_pull = jax.vjp(gelu_exact, up_proj)
    activated = activated32.astype(jnp.bfloat16)
    result = hidden + lax.psum_scatter(
        jnp.dot(activated, down_full, preferred_element_type=jnp.float32).astype(jnp.bfloat16),
        "tensor",
        scatter_dimension=0,
        tiled=True,
    ).astype(jnp.float32)
    grad_all = lax.all_gather(cotangent.astype(jnp.bfloat16), "tensor", axis=0, tiled=True)
    d_act = with_transposed(grad_all, down_full)
    d_up = gelu_pull(d_act)[0].astype(jnp.bfloat16)
    grad_down = transposed_with(activated, grad_all)
    grad_up = transposed_with(second_all, d_up)
    d_second = lax.psum_scatter(
        with_transposed(d_up, up_full).astype(jnp.bfloat16),
        "tensor",
        scatter_dimension=0,
        tiled=True,
    ).astype(jnp.float32)
    d_hidden_norm, d_gain_two, d_bias_two = norm_two_pull(d_second)
    d_hidden = cotangent + d_hidden_norm
    branch_all = lax.all_gather(d_hidden.astype(jnp.bfloat16), "tensor", axis=0, tiled=True)
    d_attended = with_transposed(branch_all, out_full).astype(jnp.bfloat16)
    grad_out = transposed_with(attended_low, branch_all)
    zeros_init = (
        jnp.zeros((heads_here, HEAD_DIM, HEAD_DIM), jnp.float32),
        jnp.zeros((heads_here, HEAD_DIM), jnp.float32),
    )
    unused_back, (d_feat_query, d_feat_key, d_vals) = lax.scan(
        block_backward,
        zeros_init,
        (
            to_blocks(feat_query),
            to_blocks(feat_key),
            to_blocks(values_low),
            to_blocks(d_attended),
            segment_blocks,
            previous_all,
            memories,
            totals_all,
        ),
        reverse=True,
    )
    d_queries = query_pull(d_feat_query.reshape(seq_len, head_cols))[0].astype(jnp.bfloat16)
    d_keys = key_pull(d_feat_key.reshape(seq_len, head_cols))[0].astype(jnp.bfloat16)
    d_values = d_vals.reshape(seq_len, head_cols).astype(jnp.bfloat16)
    grad_query = transposed_with(first_all, d_queries)
    grad_key = transposed_with(first_all, d_keys)
    grad_value = transposed_with(first_all, d_values)
    total = with_transposed(d_queries, query_full)
    total = total + with_transposed(d_keys, key_full)
    d_first = lax.psum_scatter(
        (total + with_transposed(d_values, value_full)).astype(jnp.bfloat16),
        "tensor",
        scatter_dimension=0,
        tiled=True,
    ).astype(jnp.float32)
    d_input_norm, d_gain_one, d_bias_one = norm_one_pull(d_first)
    grad_inputs = d_hidden + d_input_norm
    gain_one, bias_one, gain_two, bias_two = lax.psum(
        (d_gain_one, d_bias_one, d_gain_two, d_bias_two), ("dp", "tensor")
    )
    grad_query, grad_key, grad_value, grad_out, grad_up, grad_down = (
        lax.psum_scatter(
            grad_query.astype(jnp.bfloat16), "dp", scatter_dimension=0, tiled=True
        ).astype(jnp.float32),
        lax.psum_scatter(
            grad_key.astype(jnp.bfloat16), "dp", scatter_dimension=0, tiled=True
        ).astype(jnp.float32),
        lax.psum_scatter(
            grad_value.astype(jnp.bfloat16), "dp", scatter_dimension=0, tiled=True
        ).astype(jnp.float32),
        lax.psum_scatter(
            grad_out.astype(jnp.bfloat16), "dp", scatter_dimension=1, tiled=True
        ).astype(jnp.float32),
        lax.psum_scatter(
            grad_up.astype(jnp.bfloat16), "dp", scatter_dimension=0, tiled=True
        ).astype(jnp.float32),
        lax.psum_scatter(
            grad_down.astype(jnp.bfloat16), "dp", scatter_dimension=1, tiled=True
        ).astype(jnp.float32),
    )
    return (
        result,
        grad_inputs,
        gain_one,
        bias_one,
        gain_two,
        bias_two,
        grad_query,
        grad_key,
        grad_value,
        grad_out,
        grad_up,
        grad_down,
    )


def solution(mesh):
    in_specs = (
        P(("dp", "tensor"), None),
        P("dp", None),
        P(),
        P(),
        P(),
        P(),
        P("dp", "tensor"),
        P("dp", "tensor"),
        P("dp", "tensor"),
        P("tensor", "dp"),
        P("dp", "tensor"),
        P("tensor", "dp"),
        P(("dp", "tensor"), None),
    )
    out_specs = (
        P(("dp", "tensor"), None),
        P(("dp", "tensor"), None),
        P(),
        P(),
        P(),
        P(),
        P("dp", "tensor"),
        P("dp", "tensor"),
        P("dp", "tensor"),
        P("tensor", "dp"),
        P("dp", "tensor"),
        P("tensor", "dp"),
    )
    return jax.shard_map(local, mesh=mesh, in_specs=in_specs, out_specs=out_specs, check_vma=False)
```

profile of v0, /device:TPU:1, one launch (start us, length us, event | category | flops | bytes accessed | tf_op | source)
XLA Modules:
  0.0 1095.5 jit_solution(4512789129191410746)
XLA Ops:
  13.9 28.5 %all_gather.34 = bf16[128,1024]{0,1:T(8,128)(2,1)S(1)} all-gather(bf16[128,64]{0,1:T(8,128)(2,1)S(1)} %convert_element_type.250), channel_id=1, replica_groups=mesh['dp'=16,'tensor'=8] {'dp'}, dimensions={1}, use_global_device_ids=true | all-gather | bytes 278528 | tf_op jit(solution)/shard_map/all_gather | solution.py:157
  42.3 22.2 %all_gather.32 = bf16[1024,128]{1,0:T(8,128)(2,1)S(1)} all-gather(bf16[64,128]{1,0:T(8,128)(2,1)S(1)} %convert_element_type.244), channel_id=1, replica_groups=mesh['dp'=16,'tensor'=8] {'dp'}, dimensions={0}, use_global_device_ids=true | all-gather | bytes 278528 | tf_op jit(solution)/shard_map/all_gather | solution.py:156
  64.5 23.1 %all_gather.31 = bf16[1024,128]{1,0:T(8,128)(2,1)S(1)} all-gather(bf16[64,128]{1,0:T(8,128)(2,1)S(1)} %convert_element_type.242), channel_id=1, replica_groups=mesh['dp'=16,'tensor'=8] {'dp'}, dimensions={0}, use_global_device_ids=true | all-gather | bytes 278528 | tf_op jit(solution)/shard_map/all_gather | solution.py:155
  87.6 20.6 %all_gather.33 = bf16[1024,128]{1,0:T(8,128)(2,1)S(1)} all-gather(bf16[64,128]{1,0:T(8,128)(2,1)S(1)} %convert_element_type.246), channel_id=1, replica_groups=mesh['dp'=16,'tensor'=8] {'dp'}, dimensions={0}, use_global_device_ids=true | all-gather | bytes 278528 | tf_op jit(solution)/shard_map/all_gather | solution.py:154
  129.6 23.3 %while.44 = (s32[]{:T(128)}, f32[2,64,64]{2,1,0:T(8,128)S(1)}, f32[2,64]{1,0:T(2,128)S(1)}, s32[]{:T(128)}, bf16[4,512,2,64]{1,3,2,0:T(8,128)(2,1)S(1)}, /*index...) while((s32[]{:T(128)}, f32[2,64,64]{2,1,0:T(8,128)S(1)}, ...), condition=%wide.region_7.8_spmd.clone, body=%wide.region_4.7_spmd.clone.sunk | while | flops 574401792 | bytes 9492715 | solution.py:184
  159.1 54.5 %reduce-scatter.11.cloned.1.call-done = bf16[256,1024]{1,0:T(8,128)(2,1)} async-done(((bf16[2048,1024]{1,0:T(8,128)(2,1)}), bf16[256,1024]{1,0:T(8,128)(2,1)}) %reduce-scatter.11.cloned.1.call-update) | async-done | bytes 524304 | tf_op jit(solution)/shard_map/reduce_scatter | solution.py:190
  220.3 47.6 %all-gather.9.cloned.1.call-done = bf16[2048,1024]{1,0:T(8,128)(2,1)} async-done(((bf16[256,1024]{1,0:T(8,128)(2,1)}), bf16[2048,1024]{1,0:T(8,128)(2,1)}) %all-gather.9.cloned.1.call-update) | async-done | bytes 4194320 | tf_op jit(solution)/shard_map/all_gather | solution.py:197
  267.9 6.8 fusion.188
  274.7 40.4 %all-gather.13.cloned.1.call-done = bf16[512,1024]{0,1:T(8,128)(2,1)} async-done(((bf16[512,64]{0,1:T(8,128)(2,1)}), bf16[512,1024]{0,1:T(8,128)(2,1)}) %all-gather.13.cloned.1.call-update) | async-done | bytes 1048592 | tf_op jit(solution)/shard_map/all_gather | solution.py:159
  315.1 52.5 %all-gather.15.cloned.1.call-done = bf16[2048,1024]{1,0:T(8,128)(2,1)} async-done(((bf16[256,1024]{1,0:T(8,128)(2,1)}), bf16[2048,1024]{1,0:T(8,128)(2,1)}) %all-gather.15.cloned.1.call-update) | async-done | bytes 4194320 | tf_op jit(solution)/shard_map/all_gather | solution.py:207
  367.6 15.0 %add_convert_fusion.1 = (bf16[2048,512]{1,0:T(8,128)(2,1)S(1)}, f32[2048,512]{1,0:T(8,128)}) fusion(f32[2048,512]{1,0:T(8,128)} %fusion.188, bf16[2048,1024]{1,0:T(8,128)(2,1)} %all-gather.15.cloned.1.call-done, bf16[512,1024]{0,1:T(8,128)(2,1)} %all-gather.13.cloned.1.call-done), kind=kOutput, calls=%fused_computation.167 | convolution fusion | flops 2222981120 | bytes 15728640 | tf_op jit(solution)/shard_map/dot_general | solution.py:35
  398.9 41.6 %reduce-scatter.15.cloned.1.call-done = bf16[256,1024]{1,0:T(8,128)(2,1)} async-done(((bf16[2048,1024]{1,0:T(8,128)(2,1)}), bf16[256,1024]{1,0:T(8,128)(2,1)}) %reduce-scatter.15.cloned.1.call-update) | async-done | bytes 524304 | tf_op jit(solution)/shard_map/reduce_scatter | solution.py:212
  442.3 52.4 %reduce-scatter.13.cloned.1.call-done = bf16[256,1024]{1,0:T(8,128)(2,1)} async-done(((bf16[2048,1024]{1,0:T(8,128)(2,1)}), bf16[256,1024]{1,0:T(8,128)(2,1)}) %reduce-scatter.13.cloned.1.call-update) | async-done | bytes 524304 | tf_op jit(solution)/shard_map/reduce_scatter | solution.py:201
  499.7 6.2 convolution_convert_fusion.6
  506.0 6.4 convolution_convert_fusion.5
  512.8 38.2 %all-gather.17.cloned.1.call-done = bf16[2048,1024]{1,0:T(8,128)(2,1)} async-done(((bf16[256,1024]{1,0:T(8,128)(2,1)}), bf16[2048,1024]{1,0:T(8,128)(2,1)}) %all-gather.17.cloned.1.call-update) | async-done | bytes 4194320 | tf_op jit(solution)/shard_map/all_gather | solution.py:220
  568.0 66.0 %while.45 = (s32[]{:T(128)}, f32[2,64,64]{2,1,0:T(8,128)S(1)}, f32[2,64]{1,0:T(2,128)S(1)}, f32[4,512,2,64]{1,3,2,0:T(8,128)}, f32[4,512,2,64]{1,3,2,0:T(8,128)}...) while((s32[]{:T(128)}, f32[2,64,64]{2,1,0:T(8,128)S(1)}, ...), condition=%wide.region_18.19_spmd.clone, body=%wide.region_15.18_spmd.clone.sunk | while | flops 2340665856 | bytes 28671828 | solution.py:227
  672.4 9.0 add_convert_fusion
  690.3 66.3 %reduce-scatter.25.cloned.1.call-done = bf16[128,64]{0,1:T(8,128)(2,1)} async-done(((bf16[128,1024]{0,1:T(8,128)(2,1)}), bf16[128,64]{0,1:T(8,128)(2,1)}) %reduce-scatter.25.cloned.1.call-update) | async-done | bytes 16400 | tf_op jit(solution)/shard_map/reduce_scatter | solution.py:271
  758.0 66.5 %reduce-scatter.23.cloned.1.call-done = bf16[64,128]{1,0:T(8,128)(2,1)} async-done(((bf16[1024,128]{1,0:T(8,128)(2,1)}), bf16[64,128]{1,0:T(8,128)(2,1)}) %reduce-scatter.23.cloned.1.call-update) | async-done | bytes 16400 | tf_op jit(solution)/shard_map/reduce_scatter | solution.py:268
  825.8 66.6 %reduce-scatter.19.cloned.1.call-done = bf16[64,128]{1,0:T(8,128)(2,1)} async-done(((bf16[1024,128]{1,0:T(8,128)(2,1)}), bf16[64,128]{1,0:T(8,128)(2,1)}) %reduce-scatter.19.cloned.1.call-update) | async-done | bytes 16400 | tf_op jit(solution)/shard_map/reduce_scatter | solution.py:262
  893.8 67.0 %reduce-scatter.21.cloned.1.call-done = bf16[64,128]{1,0:T(8,128)(2,1)} async-done(((bf16[1024,128]{1,0:T(8,128)(2,1)}), bf16[64,128]{1,0:T(8,128)(2,1)}) %reduce-scatter.21.cloned.1.call-update) | async-done | bytes 16400 | tf_op jit(solution)/shard_map/reduce_scatter | solution.py:265
  962.2 54.9 %reduce-scatter.17.cloned.1.call-done = bf16[256,1024]{1,0:T(8,128)(2,1)} async-done(((bf16[2048,1024]{1,0:T(8,128)(2,1)}), bf16[256,1024]{1,0:T(8,128)(2,1)}) %reduce-scatter.17.cloned.1.call-update) | async-done | bytes 524304 | tf_op jit(solution)/shard_map/reduce_scatter | solution.py:250
  1020.1 65.0 %all-reduce = (f32[1024]{0:T(1024)}, f32[1024]{0:T(1024)}, f32[1024]{0:T(1024)}, f32[1024]{0:T(1024)}) all-reduce(f32[1024]{0:T(1024)S(1)} %get-tuple-element.509, f32[1024]{0:T(1024)S(1)} %get-tuple-element.514, f32[1024]{0:T(1024)S(1)} %get-tuple-element.511, ...), channel_id=1, replica_groups=mesh['dp'=16,'tensor'=8] {'dp','tensor'}, use_global_device_ids=true, to_apply=%region_23.24 | all-reduce | flops 4096 | bytes 32768 | tf_op jit(solution)/shard_map/psum | solution.py:258
  (347 shorter events, 216.4 us)
Async XLA Ops:
  8.1 100.1 %all-gather.7.cloned.1.call-start = ((), (), s32[]{:S(2)}) async-start(), calls=%async_computation.10 | async-start | bytes 4718592 | tf_op jit(solution)/shard_map/all_gather | solution.py:165
  13.3 200.3 %reduce-scatter.11.cloned.1.call-start = ((), (), s32[]{:S(2)}) async-start(), calls=%async_computation.11 | async-start | bytes 4718592 | tf_op jit(solution)/shard_map/reduce_scatter | solution.py:190
  13.9 98.3 %copy-start.6 = (bf16[4,512,2,64]{1,3,2,0:T(8,128)(2,1)}, bf16[4,512,2,64]{1,3,2,0:T(8,128)(2,1)S(1)}, u32[]{:S(2)}) copy-start(bf16[4,512,2,64]{1,3,2,0:T(8,128)(2,1)S(1)} %fusion.187) | copy-start | bytes 1572868
  157.5 58.3 %copy-start.28 = (f32[1024]{0:T(1024)S(1)}, f32[1024]{0:T(1024)}, u32[]{:S(2)}) copy-start(f32[1024]{0:T(1024)} %param.22) | copy-start | bytes 12292
  157.5 59.4 %copy-start.15 = (f32[512,64]{0,1:T(8,128)S(1)}, f32[512,64]{0,1:T(8,128)}, u32[]{:S(2)}) copy-start(f32[512,64]{0,1:T(8,128)} %param.28) | copy-start | bytes 393220
  157.5 62.8 %all-gather.11.cloned.1.call-start = ((), (), s32[]{:S(2)}) async-start(), calls=%async_computation.13 | async-start | bytes 1114112 | tf_op jit(solution)/shard_map/all_gather | solution.py:158
  159.1 108.9 %all-gather.9.cloned.1.call-start = ((), (), s32[]{:S(2)}) async-start(), calls=%async_computation.12 | async-start | bytes 4718592 | tf_op jit(solution)/shard_map/all_gather | solution.py:197
  216.9 98.3 %all-gather.13.cloned.1.call-start = ((), (), s32[]{:S(2)}) async-start(), calls=%async_computation.14 | async-start | bytes 1114112 | tf_op jit(solution)/shard_map/all_gather | solution.py:159
  217.6 150.0 %all-gather.15.cloned.1.call-start = ((), (), s32[]{:S(2)}) async-start(), calls=%async_computation.16 | async-start | bytes 4718592 | tf_op jit(solution)/shard_map/all_gather | solution.py:207
  219.8 220.7 %reduce-scatter.15.cloned.1.call-start = ((), (), s32[]{:S(2)}) async-start(), calls=%async_computation.17 | async-start | bytes 4718592 | tf_op jit(solution)/shard_map/reduce_scatter | solution.py:212
  388.3 106.3 %reduce-scatter.13.cloned.1.call-start = ((), (), s32[]{:S(2)}) async-start(), calls=%async_computation.15 | async-start | bytes 4718592 | tf_op jit(solution)/shard_map/reduce_scatter | solution.py:201
  398.7 152.2 %all-gather.17.cloned.1.call-start = ((), (), s32[]{:S(2)}) async-start(), calls=%async_computation.18 | async-start | bytes 4718592 | tf_op jit(solution)/shard_map/all_gather | solution.py:220
  499.6 181.9 %reduce-scatter.27.cloned.1.call-start = ((), (), s32[]{:S(2)}) async-start(), calls=%async_computation.24 | async-start | bytes 1114112 | tf_op jit(solution)/shard_map/reduce_scatter | solution.py:274
  505.9 182.9 %reduce-scatter.29.cloned.1.call-start = ((), (), s32[]{:S(2)}) async-start(), calls=%async_computation.25 | async-start | bytes 1114112 | tf_op jit(solution)/shard_map/reduce_scatter | solution.py:277
  512.4 244.2 %reduce-scatter.25.cloned.1.call-start = ((), (), s32[]{:S(2)}) async-start(), calls=%async_computation.23 | async-start | bytes 278528 | tf_op jit(solution)/shard_map/reduce_scatter | solution.py:271
  565.6 258.9 %reduce-scatter.23.cloned.1.call-start = ((), (), s32[]{:S(2)}) async-start(), calls=%async_computation.22 | async-start | bytes 278528 | tf_op jit(solution)/shard_map/reduce_scatter | solution.py:268
  646.5 246.0 %reduce-scatter.19.cloned.1.call-start = ((), (), s32[]{:S(2)}) async-start(), calls=%async_computation.20 | async-start | bytes 278528 | tf_op jit(solution)/shard_map/reduce_scatter | solution.py:262
  663.0 297.8 %reduce-scatter.21.cloned.1.call-start = ((), (), s32[]{:S(2)}) async-start(), calls=%async_computation.21 | async-start | bytes 278528 | tf_op jit(solution)/shard_map/reduce_scatter | solution.py:265
  672.3 344.7 %reduce-scatter.17.cloned.1.call-start = ((), (), s32[]{:S(2)}) async-start(), calls=%async_computation.19 | async-start | bytes 4718592 | tf_op jit(solution)/shard_map/reduce_scatter | solution.py:250
  681.4 335.6 %copy-start.16 = (f32[1024]{0:T(1024)S(1)}, f32[1024]{0:T(1024)}, u32[]{:S(2)}) copy-start(f32[1024]{0:T(1024)} %param.19) | copy-start | bytes 12292
  681.4 335.6 %copy-start.19 = (f32[256]{0:T(256)S(1)}, f32[256]{0:T(256)}, u32[]{:S(2)}) copy-start(f32[256]{0:T(256)} %copy-done.18) | copy-start | bytes 3076
  681.4 337.0 %copy-start.27 = (f32[256]{0:T(256)S(1)}, f32[256]{0:T(256)}, u32[]{:S(2)}) copy-start(f32[256]{0:T(256)} %copy-done.26) | copy-start | bytes 3076
  681.4 337.1 %copy-start.25 = (f32[256]{0:T(256)S(1)}, f32[256]{0:T(256)}, u32[]{:S(2)}) copy-start(f32[256]{0:T(256)} %copy-done.24) | copy-start | bytes 3076
  681.4 403.7 %copy-start.3 = (f32[256,1024]{1,0:T(8,128)S(1)}, f32[256,1024]{1,0:T(8,128)}, u32[]{:S(2)}) copy-start(f32[256,1024]{1,0:T(8,128)} %param.29) | copy-start | bytes 3145732
  (32 other events, 270.5 us)
Sparse Core Ops, SparseCore 0:
  13.4 59.8 all-gather.6
  157.7 55.8 reduce-scatter.10
  388.5 51.9 reduce-scatter.14
  442.8 51.8 reduce-scatter.12
Sparse Core Ops, SparseCore 1:
  161.0 48.2 all-gather.10
  217.0 50.9 all-gather.8
  270.8 44.2 all-gather.12
  316.8 50.8 all-gather.14
  499.7 51.2 all-gather.16
  554.7 64.1 reduce-scatter.26
  623.0 65.8 reduce-scatter.28
  692.4 64.2 reduce-scatter.24
  760.2 64.2 reduce-scatter.22
  828.2 64.2 reduce-scatter.18
  896.6 64.2 reduce-scatter.20
  963.3 53.7 reduce-scatter.16
where the time goes:
time: 1110 us; the launch traced here: 1100 us
  waiting for transfers between devices  655 us (59%)
  blocking collectives  159 us (14%)
  matrix products  157 us (14%)
  other arithmetic  51.6 us (5%)
  local copies, waits for them, and re-layouts  43.4 us (4%)
  between operations  16.4 us (1%)
  loops' own time  11.3 us (1%)
    reduce_scatter x1, waiting for transfers between devices, local(): lax.psum_scatter(grad_key.astype(jnp.bfloat16), 'dp', scatter_dimension=0...  67 us
    reduce_scatter x1, waiting for transfers between devices, local(): lax.psum_scatter(grad_query.astype(jnp.bfloat16), 'dp', scatter_dimension...  66.6 us
    reduce_scatter x1, waiting for transfers between devices, local(): lax.psum_scatter(grad_value.astype(jnp.bfloat16), 'dp', scatter_dimension...  66.5 us
    reduce_scatter x1, waiting for transfers between devices, local(): lax.psum_scatter(grad_out.astype(jnp.bfloat16), 'dp', scatter_dimension=1...  66.3 us
    psum x1, blocking collectives, local(): lax.psum((d_gain_one, d_bias_one, d_gain_two, d_bias_two), ('dp', 'tensor'))  65 us
    reduce_scatter x1, waiting for transfers between devices, local(): lax.psum_scatter((total + with_transposed(d_values, value_full)).astype(j...  54.9 us
    reduce_scatter x1, waiting for transfers between devices, local(): lax.psum_scatter(jnp.dot(attended_low, out_full, preferred_element_type=j...  54.5 us
    all_gather x1, waiting for transfers between devices, local(): lax.all_gather(cotangent.astype(jnp.bfloat16), 'tensor', axis=0, tiled=True)  52.5 us
  transfers between devices with their start and end apart: 16, of which 13 were waited for; matrix products, arithmetic and copies ran while one was open for 15% of the time, Pallas kernels for 0%

commit v1 on v0

v1 whole, which is shorter than its diff:
```python
import jax
import jax.numpy as jnp
from jax import lax
from jax.experimental import pallas as pl
from jax.experimental.pallas import tpu as pltpu
from jax.sharding import Mesh, PartitionSpec as P

BF = jnp.bfloat16
F32 = jnp.float32
EPS = 1e-05
BLOCK = 256
WIDTH = 1024
HALF = 512
FF_HALF = 2048
PAIRS = 4
STATE_ROWS = 80
X = ("xh", "xl")
REACH = 4


def dot(left, right, left_dim=1, right_dim=0):
    return lax.dot_general(
        left, right, (((left_dim,), (right_dim,)), ((), ())), preferred_element_type=F32
    )


def ring_shift(value, axis, step):
    return lax.ppermute(value, axis, [(i, (i + step) % 4) for i in range(4)])


def core_swap(value):
    return lax.ppermute(value, "core", [(0, 1), (1, 0)])


def turn(value, step):
    pairs = []
    for c in range(2):
        for xl in range(2):
            for y in range(4):
                pairs.append(((c * 2 + xl) * 4 + y, (xl * 2 + c) * 4 + (y + step) % 4))
    return lax.ppermute(value, ("core", "xl", "y"), pairs)


def place(pieces, index, axis=0):
    shape = list(pieces[0].shape)
    shape.insert(axis, 4)
    out = jnp.zeros(shape, pieces[0].dtype)
    for k, piece in enumerate(pieces):
        out = lax.dynamic_update_index_in_dim(out, piece, lax.rem(index - k + 4, 4), axis)
    return out


def gather_ring(value, axis, index, new_axis=0):
    return place([value] + [ring_shift(value, axis, k) for k in (1, 2, 3)], index, new_axis)


def split_pair(value):
    high = lax.reduce_precision(value, 8, 7)
    return jnp.concatenate([high, value - high], axis=0).astype(BF)


def join_pair(value):
    value = value.astype(F32)
    return value[:4] + value[4:8]


def sum_in_order(packed, index):
    return jnp.sum(place([join_pair(p) for p in packed], index), axis=0)


def scatter_ring(blocks, axis, index, block_axis=0, extra=None):
    def pick(k):
        return lax.dynamic_index_in_dim(
            blocks, lax.rem(index + k, 4), block_axis, keepdims=False
        )

    own = pick(0)
    shape, rows = own.shape, own.size // WIDTH
    total = own.astype(F32)
    if extra is not None:
        packed = jnp.concatenate([split_pair(extra), jnp.zeros((8, WIDTH), BF)], axis=0)
        extras = [packed]
    for k in (1, 2, 3):
        piece = pick(k)
        if extra is None:
            total = total + ring_shift(piece, axis, k).astype(F32)
        else:
            both = jnp.concatenate([piece.reshape(rows, WIDTH), packed], axis=0)
            both = ring_shift(both, axis, k)
            total = total + both[:rows].reshape(shape).astype(F32)
            extras.append(both[rows:])
    return total.astype(BF), None if extra is None else sum_in_order(extras, index)


def scatter_turn(blocks, index, extra=None):
    total, extras = 0.0, []
    shape, rows = blocks.shape[1:], blocks[0].size // WIDTH
    if extra is not None:
        packed = jnp.concatenate([split_pair(extra), jnp.zeros((8, WIDTH), BF)], axis=0)
    for k in range(4):
        piece = lax.dynamic_index_in_dim(blocks, lax.rem(index + k, 4), 0, keepdims=False)
        if extra is None:
            total = total + turn(piece, k).astype(F32)
        else:
            both = turn(jnp.concatenate([piece.reshape(rows, WIDTH), packed], axis=0), k)
            total = total + both[:rows].reshape(shape).astype(F32)
            extras.append(both[rows:])
    return total, None if extra is None else sum_in_order(extras, index)


def lanes(shape):
    return lax.broadcasted_iota(jnp.int32, shape, 1)


def head_sums(values):
    left = lanes(values.shape) < 64
    first = jnp.sum(jnp.where(left, values, 0.0), axis=1, keepdims=True)
    second = jnp.sum(jnp.where(left, 0.0, values), axis=1, keepdims=True)
    return jnp.where(left, first, second)


def segments_of(info, group, places):
    return sum((places >= info[group, k]).astype(jnp.int32) for k in range(4))


def column_segments(info, group):
    base = info[group, 4]
    return segments_of(info, group, base + lax.broadcasted_iota(jnp.int32, (BLOCK, 1), 0))


def pair_mask(info, group):
    base = info[group, 4]
    rows = lax.broadcasted_iota(jnp.int32, (BLOCK, 1), 0)
    cols = lax.broadcasted_iota(jnp.int32, (1, BLOCK), 1)
    row_seg = segments_of(info, group, base + rows)
    col_seg = segments_of(info, group, base + cols)
    return (rows >= cols) & (row_seg == col_seg)


def carried_of(info, group):
    return column_segments(info, group) == info[group, 5]


def in_last_of(info, group):
    return column_segments(info, group) == info[group, 6]


def pack_state(matrix, row, out):
    left = lanes((64, 128)) < 64
    out[0, 0, :64, :] = jnp.where(left, matrix[:64], matrix[64:]).astype(BF)
    out[0, 0, 64:, :] = jnp.broadcast_to(row, (STATE_ROWS - 64, 128)).astype(BF)


def unpack_state(state):
    memory = state[0, 0, :64, :].astype(F32)
    left = lanes((64, 128)) < 64
    full = jnp.concatenate(
        [jnp.where(left, memory, 0.0), jnp.where(left, 0.0, memory)], axis=0
    )
    return full.astype(BF), state[0, 0, 64:65, :].astype(F32)


def state_kernel(info, key, value, out):
    group = pl.program_id(0)
    kept = jnp.where(in_last_of(info, group), key[...].astype(F32), 0.0)
    matrix = dot(kept.astype(BF), value[...], 0, 0)
    pack_state(matrix, jnp.sum(kept, axis=0, keepdims=True), out)


def inner_kernel(info, query, key, value, numer, denom):
    group = pl.program_id(0)
    allowed = pair_mask(info, group)
    left = lanes((BLOCK, 128)) < 64
    q, k, v = query[...], key[...], value[...]
    zero = jnp.zeros_like(q)
    parts = []
    for side in (left, jnp.logical_not(left)):
        scores = jnp.where(allowed, dot(jnp.where(side, q, zero), k, 1, 1), 0.0)
        parts.append((dot(scores.astype(BF), v), jnp.sum(scores, axis=1, keepdims=True)))
    numer[...] = jnp.where(left, parts[0][0], parts[1][0])
    denom[...] = jnp.where(left, parts[0][1], parts[1][1])


def join_kernel(info, query, state, numer, denom, attended, inverse):
    group = pl.program_id(0)
    memory, totals = unpack_state(state)
    carried = carried_of(info, group)
    q = query[...]
    num = numer[...] + jnp.where(carried, dot(q, memory), 0.0)
    den = denom[...] + jnp.where(carried, head_sums(q.astype(F32) * totals), 0.0)
    inv = 1.0 / den
    attended[...] = (num * inv).astype(BF)
    inverse[...] = inv


def back_state_kernel(info, grad, attended, inverse, query, out, scaled, shift):
    group = pl.program_id(0)
    inv = inverse[...]
    d = grad[...].astype(F32)
    g = (d * inv).astype(BF)
    e = -head_sums(d * attended[...].astype(F32)) * inv
    scaled[...] = g
    shift[...] = e
    kept = jnp.where(carried_of(info, group), query[...].astype(F32), 0.0)
    pack_state(dot(kept.astype(BF), g, 0, 0), jnp.sum(kept * e, axis=0, keepdims=True), out)


def back_inner_kernel(
    info, query, key, value, scaled, shift, state, d_query, d_key, d_value
):
    group = pl.program_id(0)
    allowed = pair_mask(info, group)
    left = lanes((BLOCK, 128)) < 64
    q, k, v, g, e = query[...], key[...], value[...], scaled[...], shift[...]
    zero = jnp.zeros_like(q)
    parts = []
    for head, side in enumerate((left, jnp.logical_not(left))):
        scores = jnp.where(allowed, dot(jnp.where(side, q, zero), k, 1, 1), 0.0).astype(BF)
        d_scores = dot(jnp.where(side, g, zero), v, 1, 1) + e[:, 64 * head : 64 * head + 1]
        d_scores = jnp.where(allowed, d_scores, 0.0).astype(BF)
        parts.append((dot(d_scores, k), dot(d_scores, q, 0, 0), dot(scores, g, 0, 0)))
    dq, dk, dv = [jnp.where(left, a, b) for a, b in zip(*parts)]
    memory, totals = unpack_state(state)
    dq = dq + jnp.where(carried_of(info, group), dot(g, memory, 1, 1) + e * totals, 0.0)
    d_query[...] = (dq * jnp.minimum(q.astype(F32), 1.0)).astype(BF)
    d_key[...] = dk
    d_value[...] = dv


def back_join_kernel(info, key, value, state, d_key, d_value, key_out, value_out):
    group = pl.program_id(0)
    memory, totals = unpack_state(state)
    last = in_last_of(info, group)
    k, v = key[...], value[...]
    dk = d_key[...] + jnp.where(last, dot(v, memory, 1, 1) + totals, 0.0)
    dv = d_value[...] + jnp.where(last, dot(k, memory), 0.0)
    key_out[...] = (dk * jnp.minimum(k.astype(F32), 1.0)).astype(BF)
    value_out[...] = dv.astype(BF)


def attention_call(kernel, info, operands, outs, flops):
    def spec(shape, offset=0):
        if len(shape) == 4:
            return pl.BlockSpec((1, 1, STATE_ROWS, 128), lambda g, p: (g, p, 0, 0))
        return pl.BlockSpec((BLOCK, 128), lambda g, p: (g, p + offset))

    arrays = [a for a, _ in operands]
    moved = sum(2 * BLOCK * HALF * 4 for _ in arrays + outs)
    return pl.pallas_call(
        kernel,
        grid=(2, PAIRS),
        in_specs=[pl.BlockSpec(memory_space=pltpu.SMEM)]
        + [spec(a.shape, offset) for a, offset in operands],
        out_specs=[spec(o.shape) for o in outs],
        out_shape=outs,
        cost_estimate=pl.CostEstimate(flops=flops, bytes_accessed=moved, transcendentals=0),
        compiler_params=pltpu.CompilerParams(vmem_limit_bytes=24 * 1024 * 1024),
    )(info, *arrays)


TOKENS2 = 2 * BLOCK
STATE = jax.ShapeDtypeStruct((2, PAIRS, STATE_ROWS, 128), BF)
WIDE32 = jax.ShapeDtypeStruct((TOKENS2, HALF), F32)
WIDE16 = jax.ShapeDtypeStruct((TOKENS2, HALF), BF)


FF_STEP = 256


def gelu_parts(u):
    density = jnp.exp(-0.5 * u * u) * 0.3989422804014327
    return 0.5 * (1.0 + lax.erf(u * 0.7071067811865476)), density


def feed_kernel(second, grad, up, down, grad_up, grad_down, d_second, result, second_t, grad_t):
    step = pl.program_id(0)

    @pl.when(step == 0)
    def _():
        second_t[...] = second[...].T
        grad_t[...] = grad[...].T

    u = dot(second[...], up[...])
    d_act = dot(grad[...], down[...])
    below, density = gelu_parts(u)
    act = (u * below).astype(BF)
    d_up = (d_act * (below + u * density)).astype(BF)
    grad_up[...] = dot(second_t[...], d_up).astype(BF)
    grad_down[...] = dot(grad_t[...], act).astype(BF)
    d_part = dot(d_up, up[...], 1, 1)
    r_part = dot(act, down[...], 1, 1)

    @pl.when(step == 0)
    def _():
        d_second[...] = d_part
        result[...] = r_part

    @pl.when(step > 0)
    def _():
        d_second[...] += d_part
        result[...] += r_part


def feed_forward(second, grad, weights):
    steps = FF_HALF // FF_STEP
    whole = pl.BlockSpec((TOKENS2, WIDTH), lambda j: (0, 0))
    columns = pl.BlockSpec((WIDTH, FF_STEP), lambda j: (0, j))
    return pl.pallas_call(
        feed_kernel,
        grid=(steps,),
        in_specs=[whole, whole, columns, pl.BlockSpec((WIDTH, FF_STEP), lambda j: (0, j + steps))],
        out_specs=[columns, columns, whole, whole],
        out_shape=[
            jax.ShapeDtypeStruct((WIDTH, FF_HALF), BF),
            jax.ShapeDtypeStruct((WIDTH, FF_HALF), BF),
            jax.ShapeDtypeStruct((TOKENS2, WIDTH), F32),
            jax.ShapeDtypeStruct((TOKENS2, WIDTH), F32),
        ],
        scratch_shapes=[pltpu.VMEM((WIDTH, TOKENS2), BF), pltpu.VMEM((WIDTH, TOKENS2), BF)],
        cost_estimate=pl.CostEstimate(
            flops=12 * TOKENS2 * WIDTH * FF_HALF,
            bytes_accessed=20 * 1024 * 1024,
            transcendentals=2 * TOKENS2 * FF_HALF,
        ),
        compiler_params=pltpu.CompilerParams(vmem_limit_bytes=40 * 1024 * 1024),
    )(second, grad, weights, weights)


def norm(values, gain, bias):
    center = jnp.mean(values, axis=-1, keepdims=True)
    centred = values - center
    scale = lax.rsqrt(jnp.mean(centred * centred, axis=-1, keepdims=True) + EPS)
    unit = centred * scale
    return (unit * gain + bias).astype(BF), unit, scale


def norm_back(d_out, unit, scale, gain):
    gh = d_out * gain
    slope = scale * (
        gh
        - jnp.mean(gh, axis=-1, keepdims=True)
        - unit * jnp.mean(gh * unit, axis=-1, keepdims=True)
    )
    return slope, jnp.sum(d_out * unit, axis=0), jnp.sum(d_out, axis=0)


def both_cores(value):
    return jnp.concatenate([value, core_swap(value)], axis=0)


def sum_cores(partial):
    return partial[:BLOCK] + core_swap(partial[BLOCK:].astype(BF)).astype(F32)


def feature(values):
    return jnp.where(values > 0.0, values + 1.0, jnp.exp(jnp.minimum(values, 0.0)))


def local(
    inputs,
    lengths,
    ln1_gain,
    ln1_bias,
    ln2_gain,
    ln2_bias,
    w_query,
    w_key,
    w_value,
    w_out,
    w_up,
    w_down,
    cotangent,
):
    z = lax.axis_index("z")
    x = lax.axis_index(X)
    y = lax.axis_index("y")
    block = lax.axis_index(("xl", "y"))

    shard = jnp.concatenate(
        [w_query, w_key, w_value, w_out.T, w_up, w_down.T], axis=1
    ).astype(BF)
    turned = place([turn(shard, k) for k in range(4)], y)

    def columns(start, size):
        return jnp.concatenate([turned[j, :, start : start + size] for j in range(4)], axis=1)

    first_half = jnp.concatenate([columns(0, 128), columns(128, 128)], axis=1)
    second_half = jnp.concatenate([columns(256, 128), columns(384, 128)], axis=1)
    feed_rows = jnp.concatenate([columns(512, 512), columns(1024, 512)], axis=1)
    feed_weights = lax.all_gather(feed_rows, ("z", "xh", "xl"), axis=0, tiled=True)
    first_half = gather_ring(first_half, X, x)
    second_half = gather_ring(second_half, "z", z)
    first_half = gather_ring(first_half, "z", z).reshape(WIDTH, WIDTH)
    second_half = gather_ring(second_half, X, x, 1).reshape(WIDTH, WIDTH)

    ends = jnp.cumsum(both_cores(lengths), axis=1)

    def segment_at(place_in_group):
        return jnp.sum((place_in_group >= ends).astype(jnp.int32), axis=1)

    def last_segment(which):
        return segment_at(which * BLOCK + BLOCK - 1)

    here = last_segment(block)
    before = jnp.where(block > 0, last_segment(block - 1), -1)
    zeros = jnp.zeros((2,), jnp.int32)
    info = jnp.concatenate(
        [ends, jnp.stack([zeros + block * BLOCK, before, here, zeros], axis=1)], axis=1
    )

    first_in, unit_one, scale_one = norm(inputs, ln1_gain, ln1_bias)
    first_all = both_cores(first_in)
    grad_all = both_cores(cotangent.astype(BF))

    feats = feature(dot(first_all, first_half)).astype(BF)
    values = dot(first_all, second_half[:, :HALF]).astype(BF)
    q_, k_, v_ = (feats, 0), (feats, PAIRS), (values, 0)

    (state,) = attention_call(state_kernel, info, [k_, v_], [STATE], 2 * 256 * 128 * 128 * 8)

    def tensor_shift(value, step):
        return lax.ppermute(
            value, ("xl", "y"), [(i, i + step) for i in range(8) if 0 <= i + step < 8]
        )

    state_in = 0.0
    for k in range(1, REACH + 1):
        joined = ((block - k >= 0) & (last_segment(block - k) == before)).astype(F32)
        state_in = state_in + joined[:, None, None, None] * tensor_shift(state, k).astype(F32)
    state_in = state_in.astype(BF)

    numer, denom = attention_call(
        inner_kernel, info, [q_, k_, v_], [WIDE32, WIDE32], 4 * 2 * 256 * 256 * 128 * 8
    )
    attended, inverse = attention_call(
        join_kernel,
        info,
        [q_, (state_in, 0), (numer, 0), (denom, 0)],
        [WIDE16, WIDE32],
        2 * 256 * 128 * 128 * 8,
    )
    out_rows = second_half[:, HALF:]
    hidden = inputs + sum_cores(dot(attended, out_rows, 1, 1))

    second_in, unit_two, scale_two = norm(hidden, ln2_gain, ln2_bias)
    second_all = both_cores(second_in)
    grad_up, grad_down, d_second, ff_out = feed_forward(second_all, grad_all, feed_weights)
    result = hidden + sum_cores(ff_out)
    slope, d_gain_two, d_bias_two = norm_back(
        sum_cores(d_second), unit_two, scale_two, ln2_gain
    )
    d_hidden = cotangent + slope
    branch_all = both_cores(d_hidden.astype(BF))
    d_attended = dot(branch_all, out_rows).astype(BF)
    grad_out = dot(branch_all, attended, 0, 0).astype(BF)

    down_part, _ = scatter_ring(grad_down.reshape(4, 4, 64, FF_HALF), "z", z)
    up_part, _ = scatter_ring(grad_up.reshape(4, 4, 64, FF_HALF), X, x, 1)
    down_part, _ = scatter_ring(down_part, X, x)
    up_part, _ = scatter_ring(up_part, "z", z)
    feed_part = jnp.stack(
        [
            jnp.concatenate(
                [up_part[:, j * 512 : j * 512 + 512], down_part[:, j * 512 : j * 512 + 512]], axis=1
            )
            for j in range(4)
        ]
    )
    feed_grad, _ = scatter_turn(feed_part, y)

    back_state, scaled, shift = attention_call(
        back_state_kernel,
        info,
        [(d_attended, 0), (attended, 0), (inverse, 0), q_],
        [STATE, WIDE16, WIDE32],
        2 * 256 * 128 * 128 * 8,
    )
    state_back = 0.0
    for k in range(1, REACH + 1):
        joined = ((block + k < 8) & (last_segment(block + k - 1) == here)).astype(F32)
        state_back = state_back + joined[:, None, None, None] * tensor_shift(
            back_state, -k
        ).astype(F32)
    state_back = state_back.astype(BF)
    d_queries, d_key, d_value = attention_call(
        back_inner_kernel,
        info,
        [q_, k_, v_, (scaled, 0), (shift, 0), (state_in, 0)],
        [WIDE16, WIDE32, WIDE32],
        10 * 2 * 256 * 256 * 128 * 8,
    )
    d_keys, d_values = attention_call(
        back_join_kernel,
        info,
        [k_, v_, (state_back, 0), (d_key, 0), (d_value, 0)],
        [WIDE16, WIDE16],
        4 * 256 * 128 * 128 * 8,
    )
    d_pair = jnp.concatenate([d_queries, d_keys], axis=1)
    d_first = sum_cores(dot(d_pair, first_half, 1, 1) + dot(d_values, second_half[:, :HALF], 1, 1))
    slope, d_gain_one, d_bias_one = norm_back(d_first, unit_one, scale_one, ln1_gain)
    grad_inputs = d_hidden + slope

    norms = jnp.stack([d_gain_one, d_bias_one, d_gain_two, d_bias_two])
    packed = split_pair(norms)
    norms = join_pair(packed) + join_pair(core_swap(packed))
    grad_one = dot(first_all, d_pair, 0, 0).astype(BF)
    grad_two = jnp.concatenate([dot(first_all, d_values, 0, 0).astype(BF), grad_out], axis=1)
    one, norms = scatter_ring(grad_one.reshape(4, 4, 64, WIDTH), X, x, 1, norms)
    two, _ = scatter_ring(grad_two.reshape(4, 4, 64, WIDTH), "z", z)
    one, norms = scatter_ring(one, "z", z, 0, norms)
    two, _ = scatter_ring(two, X, x)
    part = jnp.concatenate([one, two], axis=1)
    part = part.reshape(64, 4, 4, 128).transpose(2, 0, 1, 3).reshape(4, 64, 512)
    main_grad, norms = scatter_turn(part, y, norms)

    return (
        result,
        grad_inputs,
        norms[0],
        norms[1],
        norms[2],
        norms[3],
        main_grad[:, :128],
        main_grad[:, 128:256],
        main_grad[:, 256:384],
        main_grad[:, 384:].T,
        feed_grad[:, :512],
        feed_grad[:, 512:].T,
    )


def solution(mesh):
    axes = ("z", "xh", "core", "xl", "y")
    split = Mesh(mesh.devices.reshape(4, 2, 2, 2, 4), axes)
    dp, tensor = ("z", "xh", "core"), ("xl", "y")
    tokens, rows, cols = P(axes, None), P(dp, tensor), P(tensor, dp)
    in_specs = (tokens, P(dp, None), P(), P(), P(), P(), rows, rows, rows, cols, rows, cols, tokens)
    out_specs = (tokens, tokens, P(), P(), P(), P(), rows, rows, rows, cols, rows, cols)
    return jax.shard_map(
        local, mesh=split, in_specs=in_specs, out_specs=out_specs, check_vma=False
    )
```

time: 1110 us -> 442 us (0.40)
  waiting for transfers between devices: 655 us -> 136 us
  starting transfers between devices: 1.79 us -> 166 us
  blocking collectives: 159 us -> 0 us
  matrix products: 157 us -> 9.85 us
  Pallas kernels: 0 us -> 48.3 us
  other arithmetic: 51.6 us -> 29.1 us
  local copies, waits for them, and re-layouts: 43.4 us -> 28 us
  loops' own time: 11.3 us -> 0 us
    reduce_scatter x10 -> x0, waiting for transfers between devices: 476 us -> none  [the longest x1 67 us: local(): lax.psum_scatter(grad_key.astype(jnp.bfloat16), 'dp', scatter_dimension=0...]
    all_gather x6 -> x1, waiting for transfers between devices: 179 us -> 0.01 us  [local(): lax.all_gather(feed_rows, ('z', 'xh', 'xl'), axis=0, tiled=True)]
    ppermute x0 -> x66, starting transfers between devices: none -> 165 us  [the longest x36 60.3 us: ring_shift(): return lax.ppermute(value, axis, [(i, (i + step) % 4) for i in range(4)])]
    dot_general x90 -> x9, matrix products: 157 us -> 9.85 us  [dot(): lax.dot_general(left, right, (((left_dim,), (right_dim,)), ((), ())), pre...]
    ppermute x0 -> x66, waiting for transfers between devices: none -> 136 us  [the longest x36 125 us: ring_shift(): return lax.ppermute(value, axis, [(i, (i + step) % 4) for i in range(4)])]
    all_gather x4 -> x0, blocking collectives: 94.3 us -> none  [the longest x1 28.5 us: local(): lax.all_gather(out_low, 'dp', axis=1, tiled=True)]
    psum x1 -> x0, blocking collectives: 65 us -> none  [local(): lax.psum((d_gain_one, d_bias_one, d_gain_two, d_bias_two), ('dp', 'tensor'))]
    pallas_call x0 -> x7, Pallas kernels: none -> 48.3 us  [the longest x6 26.4 us: attention_call(): pl.pallas_call(kernel, grid=(2, PAIRS), in_specs=[pl.BlockSpec(memory_spa...]
  transfers between devices with their start and end apart: 16 -> 67, of which waited for: 13 -> 25; matrix products, arithmetic and copies ran while one was open for 15% -> 10% of each run, Pallas kernels for 0% -> 6%
where the time goes in v1:
time: 442 us; the launch traced here: 433 us
  starting transfers between devices  166 us (38%)
  waiting for transfers between devices  136 us (31%)
  Pallas kernels  48.3 us (11%)
  other arithmetic  29.1 us (7%)
  local copies, waits for them, and re-layouts  28 us (6%)
  between operations  16.2 us (4%)
  matrix products  9.85 us (2%)
    ppermute x36, waiting for transfers between devices, ring_shift(): return lax.ppermute(value, axis, [(i, (i + step) % 4) for i in range(4)])  125 us
    ppermute x36, starting transfers between devices, ring_shift(): return lax.ppermute(value, axis, [(i, (i + step) % 4) for i in range(4)])  60.3 us
    ppermute x12, starting transfers between devices, turn(): return lax.ppermute(value, ('core', 'xl', 'y'), pairs)  51.3 us
    ppermute x8, starting transfers between devices, tensor_shift(): lax.ppermute(value, ('xl', 'y'), [(i, i + step) for i in range(8) if 0 <=...  34.6 us
    pallas_call x6, Pallas kernels, attention_call(): pl.pallas_call(kernel, grid=(2, PAIRS), in_specs=[pl.BlockSpec(memory_spa...  26.4 us
    pallas_call x1, Pallas kernels, feed_forward(): pl.pallas_call(feed_kernel, grid=(steps,), in_specs=[whole, whole, column...  22 us
    ppermute x10, starting transfers between devices, core_swap(): return lax.ppermute(value, 'core', [(0, 1), (1, 0)])  19.2 us
    unnamed x95, local copies, waits for them, and re-layouts  11.1 us
  transfers between devices with their start and end apart: 67, of which 25 were waited for; matrix products, arithmetic and copies ran while one was open for 10% of the time, Pallas kernels for 6%

profile of v1, /device:TPU:1, one launch (start us, length us, event | category | flops | bytes accessed | tf_op | source)
XLA Modules:
  0.0 433.2 jit_solution(13703626761590699321)
XLA Ops:
  12.2 4.5 %collective-permute-start.2 = (bf16[64,1536]{1,0:T(8,128)(2,1)S(1)}, bf16[64,1536]{1,0:T(8,128)(2,1)S(1)}, u32[]{:S(2)}, u32[]{:S(2)}) collective-permute-start(bf16[64,1536]{1,0:T(8,128)(2,1)S(1)} %constant_dynamic-update-slice_fusion), channel_id=1, source_target_pairs={{0,0},{1,1},{2,2},{3,3},{4,8},{5,9},{6,10},{7,11},{8,4},{9,5},{10,... | collective-permute-start | bytes 589832 | tf_op jit(solution)/shard_map/ppermute | solution.py:41
  17.8 4.1 collective-permute-start.4
  53.5 14.8 %collective-permute-done.15 = bf16[4,64,1024]{2,1,0:T(8,128)(2,1)S(1)} collective-permute-done((bf16[4,64,1024]{2,1,0:T(8,128)(2,1)S(1)}, bf16[4,64,1024]{2,1,0:T(8,128)(2,1)S(1)}, u32[]{:S(2)}, u32[]{:S(2)}) %collective-permute-start.15) | collective-permute-done | bytes 524320 | tf_op jit(solution)/shard_map/ppermute | solution.py:28
  68.3 10.3 %collective-permute-done.16 = bf16[4,64,1024]{2,1,0:T(8,128)(2,1)S(1)} collective-permute-done((bf16[4,64,1024]{2,1,0:T(8,128)(2,1)S(1)}, bf16[4,64,1024]{2,1,0:T(8,128)(2,1)S(1)}, u32[]{:S(2)}, u32[]{:S(2)}) %collective-permute-start.16) | collective-permute-done | bytes 524320 | tf_op jit(solution)/shard_map/ppermute | solution.py:28
  81.9 12.6 %collective-permute-done.11 = bf16[4,64,1024]{2,1,0:T(8,128)(2,1)S(1)} collective-permute-done((bf16[4,64,1024]{2,1,0:T(8,128)(2,1)S(1)}, bf16[4,64,1024]{2,1,0:T(8,128)(2,1)S(1)}, u32[]{:S(2)}, u32[]{:S(2)}) %collective-permute-start.11) | collective-permute-done | bytes 524320 | tf_op jit(solution)/shard_map/ppermute | solution.py:28
  100.6 3.8 collective-permute-start.18
  107.6 19.0 %collective-permute-start.20 = (bf16[2,4,80,128]{3,2,1,0:T(8,128)(2,1)S(1)}, bf16[2,4,80,128]{3,2,1,0:T(8,128)(2,1)S(1)}, u32[]{:S(2)}, u32[]{:S(2)}) collective-permute-start(bf16[2,4,80,128]{3,2,1,0:T(8,128)(2,1)S(1)} %shard_map.220), channel_id=1, source_target_pairs={{0,3},{1,4},{2,5},{3,6},{4,7},{8,11},{9,12},{10,13},{11,14},{12,15... | collective-permute-start | bytes 491528 | tf_op jit(solution)/shard_map/ppermute | solution.py:422
  129.9 5.6 %shard_map.221 = (f32[512,512]{1,0:T(8,128)S(1)}, f32[512,512]{1,0:T(8,128)S(1)}) custom-call(s32[2,8]{1,0:T(2,128)S(1)} %concatenate.124.info, bf16[512,1024]{1,0:T(8,128)(2,1)S(1)} %select_convert_fusion.key.query, bf16[512,1024]{1,0:T(8,128)(2,1)S(1)} %select_convert_fusion.key.query, bf16[512,512]{1,0:T(8,128)(2,1)S(1)} %convolution_convert_fusion.4.value), custom_call_target="tpu_custom_call" | custom-call | flops 536870912 | bytes 5242880 | tf_op jit(solution)/shard_map/pallas_call | solution.py:249
  139.4 4.1 collective-permute-start.22
  151.4 22.0 %shard_map.223 = (bf16[1024,2048]{1,0:T(8,128)(2,1)S(1)}, bf16[1024,2048]{1,0:T(8,128)(2,1)}, f32[512,1024]{1,0:T(8,128)S(1)}, f32[512,1024]{1,0:T(8,128)S(1)}) custom-call(bf16[512,1024]{1,0:T(8,128)(2,1)S(1)} %copy-done.6, bf16[512,1024]{1,0:T(8,128)(2,1)S(1)} %copy-done.5, bf16[1024,4096]{1,0:T(8,128)(2,1)} %all-gather.2.cloned.1.call-done.up.down, ...), custom_call_target="tpu_custom_call" | custom-call | flops 12884901888 | bytes 20971520 | tf_op jit(solution)/shard_map/pallas_call | solution.py:308
  193.9 15.3 %collective-permute-done.50 = bf16[4,64,2048]{2,1,0:T(8,128)(2,1)S(1)} collective-permute-done((bf16[4,64,2048]{2,1,0:T(8,128)(2,1)S(1)}, bf16[4,64,2048]{2,1,0:T(8,128)(2,1)S(1)}, u32[]{:S(2)}, u32[]{:S(2)}) %collective-permute-start.50) | collective-permute-done | bytes 1048608 | tf_op jit(solution)/shard_map/ppermute | solution.py:28
  209.2 4.9 %collective-permute-start.57 = (bf16[4,64,2048]{2,1,0:T(8,128)(2,1)S(1)}, bf16[4,64,2048]{2,1,0:T(8,128)(2,1)S(1)}, u32[]{:S(2)}, u32[]{:S(2)}) collective-permute-start(bf16[4,64,2048]{2,1,0:T(8,128)(2,1)S(1)} %get-tuple-element.73), channel_id=1, source_target_pairs={{0,64},{32,96},{64,0},{96,32},{1,65},{33,97},{65,1},{97,33},{2,66}... | collective-permute-start | bytes 3145736 | tf_op jit(solution)/shard_map/ppermute | solution.py:28
  218.2 13.0 %collective-permute-done.51 = bf16[4,64,2048]{2,1,0:T(8,128)(2,1)S(1)} collective-permute-done((bf16[4,64,2048]{2,1,0:T(8,128)(2,1)S(1)}, bf16[4,64,2048]{2,1,0:T(8,128)(2,1)S(1)}, u32[]{:S(2)}, u32[]{:S(2)}) %collective-permute-start.51) | collective-permute-done | bytes 1048608 | tf_op jit(solution)/shard_map/ppermute | solution.py:28
  242.6 8.4 %shard_map.225 = (bf16[512,512]{1,0:T(8,128)(2,1)S(1)}, f32[512,512]{1,0:T(8,128)S(1)}, f32[512,512]{1,0:T(8,128)S(1)}) custom-call(s32[2,8]{1,0:T(2,128)S(1)} %concatenate.124.info, bf16[512,1024]{1,0:T(8,128)(2,1)S(1)} %select_convert_fusion.key.query, bf16[512,1024]{1,0:T(8,128)(2,1)S(1)} %select_convert_fusion.key.query, ...), custom_call_target="tpu_custom_call" | custom-call | flops 1342177280 | bytes 9437184 | tf_op jit(solution)/shard_map/pallas_call | solution.py:249
  251.1 4.5 %collective-permute-start.54 = (bf16[64,2048]{1,0:T(8,128)(2,1)}, bf16[64,2048]{1,0:T(8,128)(2,1)}, u32[]{:S(2)}, u32[]{:S(2)}) collective-permute-start(bf16[64,2048]{1,0:T(8,128)(2,1)} %get-tuple-element.82), channel_id=1, source_target_pairs={{0,64},{32,96},{64,0},{96,32},{1,65},{33,97},{65,1},{97,33},{2,66}... | collective-permute-start | bytes 786440 | tf_op jit(solution)/shard_map/ppermute | solution.py:28
  257.7 10.1 %collective-permute-start.59 = (bf16[64,2048]{1,0:T(8,128)(2,1)}, bf16[64,2048]{1,0:T(8,128)(2,1)}, u32[]{:S(2)}, u32[]{:S(2)}) collective-permute-start(bf16[64,2048]{1,0:T(8,128)(2,1)} %get-tuple-element.83), channel_id=1, source_target_pairs={{0,4},{4,16},{16,20},{20,0},{1,5},{5,17},{17,21},{21,1},{2,6},{6,1... | collective-permute-start | bytes 786440 | tf_op jit(solution)/shard_map/ppermute | solution.py:28
  267.8 5.3 %collective-permute-start.60 = (bf16[64,2048]{1,0:T(8,128)(2,1)}, bf16[64,2048]{1,0:T(8,128)(2,1)}, u32[]{:S(2)}, u32[]{:S(2)}) collective-permute-start(bf16[64,2048]{1,0:T(8,128)(2,1)} %get-tuple-element.85), channel_id=1, source_target_pairs={{0,16},{4,20},{16,0},{20,4},{1,17},{5,21},{17,1},{21,5},{2,18},{6,... | collective-permute-start | bytes 786440 | tf_op jit(solution)/shard_map/ppermute | solution.py:28
  289.7 11.3 %collective-permute-start.32 = (bf16[256,1024]{1,0:T(8,128)(2,1)}, bf16[256,1024]{1,0:T(8,128)(2,1)S(1)}, u32[]{:S(2)}, u32[]{:S(2)}) collective-permute-start(bf16[256,1024]{1,0:T(8,128)(2,1)} %slice.712), channel_id=1, source_target_pairs={{0,8},{8,0},{1,9},{9,1},{2,10},{10,2},{3,11},{11,3},{4,12},{12,4},... | collective-permute-start | bytes 1572872 | tf_op jit(solution)/shard_map/ppermute | solution.py:32
  303.8 7.2 %collective-permute-start.62 = (bf16[64,1024]{1,0:T(8,128)(2,1)S(1)}, bf16[64,1024]{1,0:T(8,128)(2,1)S(1)}, u32[]{:S(2)}, u32[]{:S(2)}) collective-permute-start(bf16[64,1024]{1,0:T(8,128)(2,1)S(1)} %get-tuple-element.103), channel_id=1, source_target_pairs={{0,0},{1,1},{2,2},{3,3},{4,8},{5,9},{6,10},{7,11},{8,4},{9,5},{10,... | collective-permute-start | bytes 393224 | tf_op jit(solution)/shard_map/ppermute | solution.py:41
  311.1 22.4 %collective-permute-start.64 = (bf16[64,1024]{1,0:T(8,128)(2,1)S(1)}, bf16[64,1024]{1,0:T(8,128)(2,1)S(1)}, u32[]{:S(2)}, u32[]{:S(2)}) collective-permute-start(bf16[64,1024]{1,0:T(8,128)(2,1)S(1)} %get-tuple-element.105), channel_id=1, source_target_pairs={{0,2},{1,3},{2,0},{3,1},{4,10},{5,11},{6,8},{7,9},{8,6},{9,7},{10,... | collective-permute-start | bytes 393224 | tf_op jit(solution)/shard_map/ppermute | solution.py:41
  341.2 18.1 %collective-permute-done.40 = bf16[4,64,1024]{2,1,0:T(8,128)(2,1)S(1)} collective-permute-done((bf16[4,64,1024]{2,1,0:T(8,128)(2,1)S(1)}, bf16[4,64,1024]{2,1,0:T(8,128)(2,1)S(1)}, u32[]{:S(2)}, u32[]{:S(2)}) %collective-permute-start.40) | collective-permute-done | bytes 524320 | tf_op jit(solution)/shard_map/ppermute | solution.py:28
  369.7 24.4 %collective-permute-done.45 = bf16[64,1024]{1,0:T(8,128)(2,1)S(1)} collective-permute-done((bf16[64,1024]{1,0:T(8,128)(2,1)S(1)}, bf16[64,1024]{1,0:T(8,128)(2,1)S(1)}, u32[]{:S(2)}, u32[]{:S(2)}) %collective-permute-start.45) | collective-permute-done | bytes 131104 | tf_op jit(solution)/shard_map/ppermute | solution.py:28
  401.9 4.5 %collective-permute-done.38 = bf16[80,1024]{1,0:T(8,128)(2,1)S(1)} collective-permute-done((bf16[80,1024]{1,0:T(8,128)(2,1)S(1)}, bf16[80,1024]{1,0:T(8,128)(2,1)S(1)}, u32[]{:S(2)}, u32[]{:S(2)}) %collective-permute-start.38) | collective-permute-done | bytes 163872 | tf_op jit(solution)/shard_map/ppermute | solution.py:28
  410.8 5.5 %collective-permute-start.46 = (bf16[48,1024]{1,0:T(8,128)(2,1)S(1)}, bf16[48,1024]{1,0:T(8,128)(2,1)S(1)}, u32[]{:S(2)}, u32[]{:S(2)}) collective-permute-start(bf16[48,1024]{1,0:T(8,128)(2,1)S(1)} %get-tuple-element.134), channel_id=1, source_target_pairs={{0,0},{1,1},{2,2},{3,3},{4,8},{5,9},{6,10},{7,11},{8,4},{9,5},{10,... | collective-permute-start | bytes 294920 | tf_op jit(solution)/shard_map/ppermute | solution.py:41
  (376 shorter events, 161.4 us)
Async XLA Ops:
  7.2 141.8 %all-gather.2.cloned.1.call-start = ((), (), s32[]{:S(2)}) async-start(), calls=%async_computation | async-start | bytes 8912896 | tf_op jit(solution)/shard_map/all_gather | solution.py:390
  30.1 64.5 %collective-permute-start.1 = (bf16[256,1024]{1,0:T(8,128)(2,1)S(1)}, bf16[256,1024]{1,0:T(8,128)(2,1)S(1)}, u32[]{:S(2)}, u32[]{:S(2)}) collective-permute-start(bf16[256,1024]{1,0:T(8,128)(2,1)S(1)} %add_convert_fusion.1), channel_id=1, source_target_pairs={{0,8},{8,0},{1,9},{9,1},{2,10},{10,2},{3,11},{11,3},{4,12},{12,4},... | collective-permute-start | bytes 1572872 | tf_op jit(solution)/shard_map/ppermute | solution.py:32
  46.2 32.4 %collective-permute-start.16 = (bf16[4,64,1024]{2,1,0:T(8,128)(2,1)S(1)}, bf16[4,64,1024]{2,1,0:T(8,128)(2,1)S(1)}, u32[]{:S(2)}, u32[]{:S(2)}) collective-permute-start(bf16[4,64,1024]{2,1,0:T(8,128)(2,1)S(1)} %bitcast_dynamic-update-slice_fusion.12), channel_id=1, source_target_pairs={{0,16},{4,20},{16,0},{20,4},{1,17},{5,21},{17,1},{21,5},{2,18},{6,... | collective-permute-start | bytes 1572872 | tf_op jit(solution)/shard_map/ppermute | solution.py:28
  49.1 31.0 %collective-permute-start.17 = (bf16[4,64,1024]{2,1,0:T(8,128)(2,1)S(1)}, bf16[4,64,1024]{2,1,0:T(8,128)(2,1)S(1)}, u32[]{:S(2)}, u32[]{:S(2)}) collective-permute-start(bf16[4,64,1024]{2,1,0:T(8,128)(2,1)S(1)} %bitcast_dynamic-update-slice_fusion.12), channel_id=1, source_target_pairs={{0,20},{4,0},{16,4},{20,16},{1,21},{5,1},{17,5},{21,17},{2,22},{6,... | collective-permute-start | bytes 1572872 | tf_op jit(solution)/shard_map/ppermute | solution.py:28
  53.1 27.1 %collective-permute-start.9 = (bf16[4,64,1024]{2,1,0:T(8,128)(2,1)S(1)}, bf16[4,64,1024]{2,1,0:T(8,128)(2,1)S(1)}, u32[]{:S(2)}, u32[]{:S(2)}) collective-permute-start(bf16[4,64,1024]{2,1,0:T(8,128)(2,1)S(1)} %bitcast_dynamic-update-slice_fusion.16), channel_id=1, source_target_pairs={{0,32},{32,64},{64,96},{96,0},{1,33},{33,65},{65,97},{97,1},{2,34}... | collective-permute-start | bytes 1572872 | tf_op jit(solution)/shard_map/ppermute | solution.py:28
  100.6 34.9 %collective-permute-start.18 = (bf16[2,4,80,128]{3,2,1,0:T(8,128)(2,1)S(1)}, bf16[2,4,80,128]{3,2,1,0:T(8,128)(2,1)S(1)}, u32[]{:S(2)}, u32[]{:S(2)}) collective-permute-start(bf16[2,4,80,128]{3,2,1,0:T(8,128)(2,1)S(1)} %shard_map.220), channel_id=1, source_target_pairs={{0,1},{1,2},{2,3},{3,4},{4,5},{5,6},{6,7},{8,9},{9,10},{10,11},{11... | collective-permute-start | bytes 491528 | tf_op jit(solution)/shard_map/ppermute | solution.py:422
  104.5 31.1 %collective-permute-start.19 = (bf16[2,4,80,128]{3,2,1,0:T(8,128)(2,1)S(1)}, bf16[2,4,80,128]{3,2,1,0:T(8,128)(2,1)S(1)}, u32[]{:S(2)}, u32[]{:S(2)}) collective-permute-start(bf16[2,4,80,128]{3,2,1,0:T(8,128)(2,1)S(1)} %shard_map.220), channel_id=1, source_target_pairs={{0,2},{1,3},{2,4},{3,5},{4,6},{5,7},{8,10},{9,11},{10,12},{11,13},... | collective-permute-start | bytes 491528 | tf_op jit(solution)/shard_map/ppermute | solution.py:422
  107.6 27.9 %collective-permute-start.20 = (bf16[2,4,80,128]{3,2,1,0:T(8,128)(2,1)S(1)}, bf16[2,4,80,128]{3,2,1,0:T(8,128)(2,1)S(1)}, u32[]{:S(2)}, u32[]{:S(2)}) collective-permute-start(bf16[2,4,80,128]{3,2,1,0:T(8,128)(2,1)S(1)} %shard_map.220), channel_id=1, source_target_pairs={{0,3},{1,4},{2,5},{3,6},{4,7},{8,11},{9,12},{10,13},{11,14},{12,15... | collective-permute-start | bytes 491528 | tf_op jit(solution)/shard_map/ppermute | solution.py:422
  183.4 47.8 %collective-permute-start.51 = (bf16[4,64,2048]{2,1,0:T(8,128)(2,1)S(1)}, bf16[4,64,2048]{2,1,0:T(8,128)(2,1)S(1)}, u32[]{:S(2)}, u32[]{:S(2)}) collective-permute-start(bf16[4,64,2048]{2,1,0:T(8,128)(2,1)S(1)} %get-tuple-element.70), channel_id=1, source_target_pairs={{0,16},{4,20},{16,0},{20,4},{1,17},{5,21},{17,1},{21,5},{2,18},{6,... | collective-permute-start | bytes 3145736 | tf_op jit(solution)/shard_map/ppermute | solution.py:28
  185.6 46.9 %collective-permute-start.52 = (bf16[4,64,2048]{2,1,0:T(8,128)(2,1)S(1)}, bf16[4,64,2048]{2,1,0:T(8,128)(2,1)S(1)}, u32[]{:S(2)}, u32[]{:S(2)}) collective-permute-start(bf16[4,64,2048]{2,1,0:T(8,128)(2,1)S(1)} %get-tuple-element.69), channel_id=1, source_target_pairs={{0,20},{4,0},{16,4},{20,16},{1,21},{5,1},{17,5},{21,17},{2,22},{6,... | collective-permute-start | bytes 3145736 | tf_op jit(solution)/shard_map/ppermute | solution.py:28
  193.8 43.1 %collective-permute-start.56 = (bf16[4,64,2048]{2,1,0:T(8,128)(2,1)S(1)}, bf16[4,64,2048]{2,1,0:T(8,128)(2,1)S(1)}, u32[]{:S(2)}, u32[]{:S(2)}) collective-permute-start(bf16[4,64,2048]{2,1,0:T(8,128)(2,1)S(1)} %get-tuple-element.71), channel_id=1, source_target_pairs={{0,32},{32,64},{64,96},{96,0},{1,33},{33,65},{65,97},{97,1},{2,34}... | collective-permute-start | bytes 3145736 | tf_op jit(solution)/shard_map/ppermute | solution.py:28
  209.2 29.1 %collective-permute-start.57 = (bf16[4,64,2048]{2,1,0:T(8,128)(2,1)S(1)}, bf16[4,64,2048]{2,1,0:T(8,128)(2,1)S(1)}, u32[]{:S(2)}, u32[]{:S(2)}) collective-permute-start(bf16[4,64,2048]{2,1,0:T(8,128)(2,1)S(1)} %get-tuple-element.73), channel_id=1, source_target_pairs={{0,64},{32,96},{64,0},{96,32},{1,65},{33,97},{65,1},{97,33},{2,66}... | collective-permute-start | bytes 3145736 | tf_op jit(solution)/shard_map/ppermute | solution.py:28
  238.3 29.5 %collective-permute-start.31 = (bf16[2,4,80,128]{3,2,1,0:T(8,128)(2,1)S(1)}, bf16[2,4,80,128]{3,2,1,0:T(8,128)(2,1)S(1)}, u32[]{:S(2)}, u32[]{:S(2)}) collective-permute-start(bf16[2,4,80,128]{3,2,1,0:T(8,128)(2,1)S(1)} %get-tuple-element.37), channel_id=1, source_target_pairs={{4,0},{5,1},{6,2},{7,3},{12,8},{13,9},{14,10},{15,11},{20,16},{21,... | collective-permute-start | bytes 491528 | tf_op jit(solution)/shard_map/ppermute | solution.py:422
  239.6 50.0 %collective-permute-start.53 = (bf16[64,2048]{1,0:T(8,128)(2,1)}, bf16[64,2048]{1,0:T(8,128)(2,1)}, u32[]{:S(2)}, u32[]{:S(2)}) collective-permute-start(bf16[64,2048]{1,0:T(8,128)(2,1)} %get-tuple-element.80), channel_id=1, source_target_pairs={{0,32},{32,64},{64,96},{96,0},{1,33},{33,65},{65,97},{97,1},{2,34}... | collective-permute-start | bytes 786440 | tf_op jit(solution)/shard_map/ppermute | solution.py:28
  251.1 38.6 %collective-permute-start.54 = (bf16[64,2048]{1,0:T(8,128)(2,1)}, bf16[64,2048]{1,0:T(8,128)(2,1)}, u32[]{:S(2)}, u32[]{:S(2)}) collective-permute-start(bf16[64,2048]{1,0:T(8,128)(2,1)} %get-tuple-element.82), channel_id=1, source_target_pairs={{0,64},{32,96},{64,0},{96,32},{1,65},{33,97},{65,1},{97,33},{2,66}... | collective-permute-start | bytes 786440 | tf_op jit(solution)/shard_map/ppermute | solution.py:28
  255.7 45.3 %collective-permute-start.55 = (bf16[64,2048]{1,0:T(8,128)(2,1)S(1)}, bf16[64,2048]{1,0:T(8,128)(2,1)}, u32[]{:S(2)}, u32[]{:S(2)}) collective-permute-start(bf16[64,2048]{1,0:T(8,128)(2,1)S(1)} %get-tuple-element.81), channel_id=1, source_target_pairs={{0,96},{32,0},{64,32},{96,64},{1,97},{33,1},{65,33},{97,65},{2,98}... | collective-permute-start | bytes 786440 | tf_op jit(solution)/shard_map/ppermute | solution.py:28
  257.7 44.6 %collective-permute-start.59 = (bf16[64,2048]{1,0:T(8,128)(2,1)}, bf16[64,2048]{1,0:T(8,128)(2,1)}, u32[]{:S(2)}, u32[]{:S(2)}) collective-permute-start(bf16[64,2048]{1,0:T(8,128)(2,1)} %get-tuple-element.83), channel_id=1, source_target_pairs={{0,4},{4,16},{16,20},{20,0},{1,5},{5,17},{17,21},{21,1},{2,6},{6,1... | collective-permute-start | bytes 786440 | tf_op jit(solution)/shard_map/ppermute | solution.py:28
  267.8 34.6 %collective-permute-start.60 = (bf16[64,2048]{1,0:T(8,128)(2,1)}, bf16[64,2048]{1,0:T(8,128)(2,1)}, u32[]{:S(2)}, u32[]{:S(2)}) collective-permute-start(bf16[64,2048]{1,0:T(8,128)(2,1)} %get-tuple-element.85), channel_id=1, source_target_pairs={{0,16},{4,20},{16,0},{20,4},{1,17},{5,21},{17,1},{21,5},{2,18},{6,... | collective-permute-start | bytes 786440 | tf_op jit(solution)/shard_map/ppermute | solution.py:28
  289.7 50.4 %collective-permute-start.32 = (bf16[256,1024]{1,0:T(8,128)(2,1)}, bf16[256,1024]{1,0:T(8,128)(2,1)S(1)}, u32[]{:S(2)}, u32[]{:S(2)}) collective-permute-start(bf16[256,1024]{1,0:T(8,128)(2,1)} %slice.712), channel_id=1, source_target_pairs={{0,8},{8,0},{1,9},{9,1},{2,10},{10,2},{3,11},{11,3},{4,12},{12,4},... | collective-permute-start | bytes 1572872 | tf_op jit(solution)/shard_map/ppermute | solution.py:32
  303.8 30.1 %collective-permute-start.62 = (bf16[64,1024]{1,0:T(8,128)(2,1)S(1)}, bf16[64,1024]{1,0:T(8,128)(2,1)S(1)}, u32[]{:S(2)}, u32[]{:S(2)}) collective-permute-start(bf16[64,1024]{1,0:T(8,128)(2,1)S(1)} %get-tuple-element.103), channel_id=1, source_target_pairs={{0,0},{1,1},{2,2},{3,3},{4,8},{5,9},{6,10},{7,11},{8,4},{9,5},{10,... | collective-permute-start | bytes 393224 | tf_op jit(solution)/shard_map/ppermute | solution.py:41
  311.1 26.5 %collective-permute-start.64 = (bf16[64,1024]{1,0:T(8,128)(2,1)S(1)}, bf16[64,1024]{1,0:T(8,128)(2,1)S(1)}, u32[]{:S(2)}, u32[]{:S(2)}) collective-permute-start(bf16[64,1024]{1,0:T(8,128)(2,1)S(1)} %get-tuple-element.105), channel_id=1, source_target_pairs={{0,2},{1,3},{2,0},{3,1},{4,10},{5,11},{6,8},{7,9},{8,6},{9,7},{10,... | collective-permute-start | bytes 393224 | tf_op jit(solution)/shard_map/ppermute | solution.py:41
  362.7 31.4 %collective-permute-start.34 = (bf16[272,1024]{1,0:T(8,128)(2,1)S(1)}, bf16[272,1024]{1,0:T(8,128)(2,1)S(1)}, u32[]{:S(2)}, u32[]{:S(2)}) collective-permute-start(bf16[272,1024]{1,0:T(8,128)(2,1)S(1)} %get-tuple-element.140), channel_id=1, source_target_pairs={{0,4},{4,16},{16,20},{20,0},{1,5},{5,17},{17,21},{21,1},{2,6},{6,1... | collective-permute-start | bytes 1671176 | tf_op jit(solution)/shard_map/ppermute | solution.py:28
  364.3 29.9 %collective-permute-start.35 = (bf16[272,1024]{1,0:T(8,128)(2,1)S(1)}, bf16[272,1024]{1,0:T(8,128)(2,1)S(1)}, u32[]{:S(2)}, u32[]{:S(2)}) collective-permute-start(bf16[272,1024]{1,0:T(8,128)(2,1)S(1)} %get-tuple-element.139), channel_id=1, source_target_pairs={{0,16},{4,20},{16,0},{20,4},{1,17},{5,21},{17,1},{21,5},{2,18},{6,... | collective-permute-start | bytes 1671176 | tf_op jit(solution)/shard_map/ppermute | solution.py:28
  366.0 28.3 %collective-permute-start.36 = (bf16[272,1024]{1,0:T(8,128)(2,1)S(1)}, bf16[272,1024]{1,0:T(8,128)(2,1)S(1)}, u32[]{:S(2)}, u32[]{:S(2)}) collective-permute-start(bf16[272,1024]{1,0:T(8,128)(2,1)S(1)} %get-tuple-element.138), channel_id=1, source_target_pairs={{0,20},{4,0},{16,4},{20,16},{1,21},{5,1},{17,5},{21,17},{2,22},{6,... | collective-permute-start | bytes 1671176 | tf_op jit(solution)/shard_map/ppermute | solution.py:28
  (83 other events, 858.9 us)
Sparse Core Ops, SparseCore 0:
  29.5 99.9 all-gather.1
